TPU v7x, 32 devices: a whole 2x2x4 slice. The times are simulated.
32 devices in a mesh: blk: 4 (over y, x), dom: 8 (over z, core).
Axes of the slice: x: 2, y: 2, z: 4, core: 2. Of those that a mesh axis runs over, the one named last changes fastest.
Arguments:
- source_emb: bfloat16 [4096, 64], P(('blk', 'dom')), may hold values from -6 to 6
- target_emb: bfloat16 [24576, 64], P(('blk', 'dom')), may hold values from -6 to 6
- source_counts: int32 [4096, 128], P(('blk', 'dom')), may hold values from 1 to 4
- target_counts: int32 [24576, 128], P(('blk', 'dom')), may hold values from 1 to 4
- warm_start: float32 [24576, 128], P(('blk', 'dom')), may hold values from -8 to 263
Outputs:
- source_log_scaling: float32 [4096, 128], P(('blk', 'dom'))
- target_log_scaling: float32 [24576, 128], P(('blk', 'dom'))
All inputs are finite; a program needn't handle non-finite values.
Results may differ from a plain program's by a relative error of at most 0.0022.
Values may be sent and summed in bfloat16 or wider, within the bound.
A program may use at most 64 MiB of HBM per device.

v0:
```python
import math

import jax
import jax.numpy as jnp
from jax import lax
from jax.sharding import PartitionSpec as P

ITERS = 2


entropic = 0.05


def normalized(values):
    widened = values.astype(jnp.float32)
    squared = jnp.sum(widened * widened, axis=1, keepdims=True) + 1e-06
    return (widened * lax.rsqrt(squared)).astype(jnp.bfloat16)


def block_rows(count, largest):
    if count <= largest:
        return count
    return math.gcd(count, largest)


def kernel_sums(row_emb, col_emb, col_weights):
    row_count = row_emb.shape[0]
    col_count = col_emb.shape[0]
    row_block = block_rows(row_count, 1024)
    col_block = block_rows(col_count, 2048)
    row_parts = row_emb.reshape(row_count // row_block, row_block, row_emb.shape[1])
    col_parts = col_emb.reshape(col_count // col_block, col_block, col_emb.shape[1])
    weight_parts = col_weights.reshape(col_count // col_block, col_block, col_weights.shape[1])

    def one_block(row_piece):

        def add_block(running, paired):
            col_piece, weight_piece = paired
            products = jnp.dot(row_piece, col_piece.T, preferred_element_type=jnp.float32)
            kernel = jnp.exp((products - 1.0) / entropic).astype(jnp.bfloat16)
            return (
                running + jnp.dot(kernel, weight_piece, preferred_element_type=jnp.float32),
                None,
            )

        initial = jnp.zeros((row_piece.shape[0], col_weights.shape[1]), jnp.float32)
        result, unused = lax.scan(add_block, initial, (col_parts, weight_parts))
        return result

    return lax.map(one_block, row_parts).reshape(row_count, col_weights.shape[1])


def column_peak(values):
    return lax.pmax(jnp.max(values, axis=0), ("blk", "dom"))


def body(source_emb, target_emb, source_counts, target_counts, warm_start):
    blk_count = lax.axis_size("blk")
    dom_count = lax.axis_size("dom")
    src_rows = source_emb.shape[0]
    tgt_rows = target_emb.shape[0]
    columns = warm_start.shape[1]
    all_sources = src_rows * blk_count * dom_count
    all_targets = tgt_rows * blk_count * dom_count
    source_block = lax.all_gather(normalized(source_emb), "dom", axis=0, tiled=True)
    own_targets = normalized(target_emb)
    target_group = lax.all_gather(own_targets, "blk", axis=0, tiled=True)
    log_target = jnp.log(target_counts.astype(jnp.float32)) - math.log(all_targets)
    log_source = jnp.log(source_counts.astype(jnp.float32)) - math.log(all_sources)
    target_logs = warm_start
    source_logs = jnp.zeros((src_rows, columns), jnp.float32)
    for iteration in range(ITERS):
        target_peak = column_peak(target_logs)
        scaled = jnp.exp(target_logs - target_peak).astype(jnp.bfloat16)
        partial_value = kernel_sums(
            source_block, target_group, lax.all_gather(scaled, "blk", axis=0, tiled=True)
        )
        shares = lax.psum_scatter(partial_value, "dom", scatter_dimension=0, tiled=True)
        source_logs = log_source - target_peak - jnp.log(shares)
        source_peak = column_peak(source_logs)
        block_logs = lax.all_gather(source_logs, "dom", axis=0, tiled=True)
        weights = jnp.exp(block_logs - source_peak).astype(jnp.bfloat16)
        target_sums = kernel_sums(
            own_targets,
            lax.all_gather(source_block, "blk", axis=0, tiled=True),
            lax.all_gather(weights, "blk", axis=0, tiled=True),
        )
        target_logs = log_target - source_peak - jnp.log(target_sums)
    return (source_logs, target_logs)


def solution(mesh):
    in_specs = (
        P(("blk", "dom"), None),
        P(("blk", "dom"), None),
        P(("blk", "dom"), None),
        P(("blk", "dom"), None),
        P(("blk", "dom"), None),
    )
    out_specs = (P(("blk", "dom"), None), P(("blk", "dom"), None))
    return jax.shard_map(body, mesh=mesh, in_specs=in_specs, out_specs=out_specs, check_vma=False)
```

profile of v0, /device:TPU:1, one launch (start us, length us, event | category | flops | bytes accessed | tf_op | source)
XLA Modules:
  0.0 395.5 jit_solution(12074339199688182568)
XLA Ops:
  8.7 10.2 %all_gather.28 = bf16[3072,64]{1,0:T(8,128)(2,1)S(1)} all-gather(bf16[768,64]{1,0:T(8,128)(2,1)S(1)} %fusion.49), channel_id=1, replica_groups=mesh['blk'=4,'dom'=8] {'blk'}, dimensions={0}, use_global_device_ids=true | all-gather | bytes 491520 | tf_op jit(solution)/shard_map/all_gather | solution.py:67
  19.0 15.4 %all_gather.29 = bf16[1024,64]{0,1:T(8,128)(2,1)S(1)} all-gather(bf16[128,64]{0,1:T(8,128)(2,1)S(1)} %fusion.52), channel_id=1, replica_groups=mesh['blk'=4,'dom'=8] {'dom'}, dimensions={0}, use_global_device_ids=true | all-gather | bytes 147456 | tf_op jit(solution)/shard_map/all_gather | solution.py:65
  34.6 38.0 %pmax.28 = f32[128]{0:T(128)S(1)} all-reduce(f32[128]{0:T(128)S(1)} %reduce_max.36), channel_id=1, replica_groups=mesh['blk'=4,'dom'=8] {'blk','dom'}, use_global_device_ids=true, to_apply=%region_1.0 | all-reduce | flops 128 | bytes 1024 | tf_op jit(solution)/shard_map/pmax | solution.py:54
  72.7 10.6 %all_gather.30 = bf16[3072,128]{1,0:T(8,128)(2,1)S(1)} all-gather(bf16[768,128]{1,0:T(8,128)(2,1)S(1)} %exponential_convert_fusion.7), channel_id=1, replica_groups=mesh['blk'=4,'dom'=8] {'blk'}, dimensions={0}, use_global_device_ids=true | all-gather | bytes 983040 | tf_op jit(solution)/shard_map/all_gather | solution.py:76
  83.3 4.6 %while.80 = (s32[]{:T(128)}, f32[1024,128]{1,0:T(8,128)S(1)}, bf16[3,1024,64]{2,1,0:T(8,128)(2,1)S(1)}, bf16[1024,64]{1,0:T(8,128)(2,1)S(1)}, bf16[3,1024,128]{2,1,0:T(8,128)(2,1)S(1)}, /*index=5*/s32[]{:T(128)}, s32[]{:T(128)}) while((s32[]{:T(128)}, f32[1024,128]{1,0:T(8,128)S(1)}, bf16[3,1024,64]{2,1,0:T(8,128)(2,1)S(1)}, ...), condition=%wide.region_5.6_spmd.clone, body=%wide.region_4.5_spmd.clone.sunk | while | flops 406061056 | bytes 1836119 | solution.py:47
  88.7 28.7 %reduce-scatter.3.cloned.1.call-done = f32[128,128]{1,0:T(8,128)} async-done(((f32[1024,128]{1,0:T(8,128)}), f32[128,128]{1,0:T(8,128)}) %reduce-scatter.3.cloned.1.call-update) | async-done | bytes 65552 | tf_op jit(solution)/shard_map/reduce_scatter | solution.py:78
  118.4 40.4 %pmax.29 = f32[128]{0:T(128)S(1)} all-reduce(f32[128]{0:T(128)S(1)} %get-tuple-element.460), channel_id=1, replica_groups=mesh['blk'=4,'dom'=8] {'blk','dom'}, use_global_device_ids=true, to_apply=%region_8.9 | all-reduce | flops 128 | bytes 1024 | tf_op jit(solution)/shard_map/pmax | solution.py:54
  158.8 16.9 %all_gather.32 = f32[1024,128]{1,0:T(8,128)S(1)} all-gather(f32[128,128]{1,0:T(8,128)S(1)} %get-tuple-element.461), channel_id=1, replica_groups=mesh['blk'=4,'dom'=8] {'dom'}, dimensions={0}, use_global_device_ids=true | all-gather | bytes 589824 | tf_op jit(solution)/shard_map/all_gather | solution.py:81
  176.5 9.8 %all_gather.31 = bf16[4096,64]{0,1:T(8,128)(2,1)S(1)} all-gather(bf16[1024,64]{0,1:T(8,128)(2,1)S(1)} %all_gather.29), channel_id=1, replica_groups=mesh['blk'=4,'dom'=8] {'blk'}, dimensions={0}, use_global_device_ids=true | all-gather | bytes 655360 | tf_op jit(solution)/shard_map/all_gather | solution.py:85
  186.8 15.8 %all-gather.3.cloned.1.call-done = bf16[4096,128]{1,0:T(8,128)(2,1)} async-done(((bf16[1024,128]{1,0:T(8,128)(2,1)}), bf16[4096,128]{1,0:T(8,128)(2,1)}) %all-gather.3.cloned.1.call-update) | async-done | bytes 1048592 | tf_op jit(solution)/shard_map/all_gather | solution.py:86
  202.6 6.4 %while.81 = (s32[]{:T(128)}, f32[768,128]{1,0:T(8,128)S(1)}, bf16[2,2048,64]{2,1,0:T(8,128)(2,1)S(1)}, bf16[768,64]{1,0:T(8,128)(2,1)S(1)}, bf16[2,2048,128]{2,1,0:T(8,128)(2,1)}, /*index=5*/s32[]{:T(128)}, s32[]{:T(128)}) while((s32[]{:T(128)}, f32[768,128]{1,0:T(8,128)S(1)}, bf16[2,2048,64]{2,1,0:T(8,128)(2,1)S(1)}, ...), condition=%wide.region_10.11_spmd.clone, body=%wide.region_9.10_spmd.clone.sunk | while | flops 608894976 | bytes 2032727 | solution.py:47
  202.6 3.2 fusion.82
  205.8 3.2 fusion.82
  209.2 38.5 %pmax.30 = f32[128]{0:T(128)S(1)} all-reduce(f32[128]{0:T(128)S(1)} %fusion.50), channel_id=1, replica_groups=mesh['blk'=4,'dom'=8] {'blk','dom'}, use_global_device_ids=true, to_apply=%region_12.13 | all-reduce | flops 128 | bytes 1024 | tf_op jit(solution)/shard_map/pmax | solution.py:54
  247.9 10.6 %all_gather.34 = bf16[3072,128]{1,0:T(8,128)(2,1)S(1)} all-gather(bf16[768,128]{1,0:T(8,128)(2,1)S(1)} %exponential_convert_fusion.6), channel_id=1, replica_groups=mesh['blk'=4,'dom'=8] {'blk'}, dimensions={0}, use_global_device_ids=true | all-gather | bytes 983040 | tf_op jit(solution)/shard_map/all_gather | solution.py:76
  258.5 7.4 %while.82 = (s32[]{:T(128)}, f32[1024,128]{1,0:T(8,128)S(1)}, bf16[3,1024,64]{2,1,0:T(8,128)(2,1)S(1)}, bf16[1024,64]{1,0:T(8,128)(2,1)}, bf16[3,1024,128]{2,1,0:T(8,128)(2,1)S(1)}, /*index=5*/s32[]{:T(128)}, s32[]{:T(128)}) while((s32[]{:T(128)}, f32[1024,128]{1,0:T(8,128)S(1)}, bf16[3,1024,64]{2,1,0:T(8,128)(2,1)S(1)}, ...), condition=%wide.region_14.15_spmd.clone, body=%wide.region_13.14_spmd.clone.sunk | while | flops 406061056 | bytes 1836119 | solution.py:47
  258.5 2.5 fusion.86
  266.9 29.3 %reduce-scatter.5.cloned.1.call-done = f32[128,128]{1,0:T(8,128)} async-done(((f32[1024,128]{1,0:T(8,128)}), f32[128,128]{1,0:T(8,128)}) %reduce-scatter.5.cloned.1.call-update) | async-done | bytes 65552 | tf_op jit(solution)/shard_map/reduce_scatter | solution.py:78
  297.1 19.0 %all_gather.35 = f32[1024,128]{1,0:T(8,128)S(1)} all-gather(f32[128,128]{1,0:T(8,128)S(1)} %get-tuple-element.459), channel_id=1, replica_groups=mesh['blk'=4,'dom'=8] {'dom'}, dimensions={0}, use_global_device_ids=true | all-gather | bytes 589824 | tf_op jit(solution)/shard_map/all_gather | solution.py:81
  316.1 37.4 %pmax.31 = f32[128]{0:T(128)S(1)} all-reduce(f32[128]{0:T(128)S(1)} %get-tuple-element.458), channel_id=1, replica_groups=mesh['blk'=4,'dom'=8] {'blk','dom'}, use_global_device_ids=true, to_apply=%region_17.18 | all-reduce | flops 128 | bytes 1024 | tf_op jit(solution)/shard_map/pmax | solution.py:54
  354.3 27.3 %all-gather.5.cloned.1.call-done = bf16[4096,128]{1,0:T(8,128)(2,1)} async-done(((bf16[1024,128]{1,0:T(8,128)(2,1)}), bf16[4096,128]{1,0:T(8,128)(2,1)}) %all-gather.5.cloned.1.call-update) | async-done | bytes 1048592 | tf_op jit(solution)/shard_map/all_gather | solution.py:86
  381.7 6.4 %while.83 = (s32[]{:T(128)}, f32[768,128]{1,0:T(8,128)S(1)}, bf16[2,2048,64]{2,1,0:T(8,128)(2,1)S(1)}, bf16[768,64]{1,0:T(8,128)(2,1)S(1)}, bf16[2,2048,128]{2,1,0:T(8,128)(2,1)}, /*index=5*/s32[]{:T(128)}, s32[]{:T(128)}) while((s32[]{:T(128)}, f32[768,128]{1,0:T(8,128)S(1)}, bf16[2,2048,64]{2,1,0:T(8,128)(2,1)S(1)}, ...), condition=%wide.region_19.20_spmd.clone, body=%wide.region_18.19_spmd.clone.sunk | while | flops 608894976 | bytes 2032727 | solution.py:47
  381.7 3.2 fusion.90
  384.9 3.2 fusion.90
  (57 shorter events, 18.1 us)
Async XLA Ops:
  7.2 11.8 %copy-start.10 = (bf16[128,64]{0,1:T(8,128)(2,1)S(1)}, bf16[128,64]{0,1:T(8,128)(2,1)}, u32[]{:S(2)}) copy-start(bf16[128,64]{0,1:T(8,128)(2,1)} %param.13) | copy-start | bytes 49156
  7.2 110.3 %reduce-scatter.3.cloned.1.call-start = ((), (), s32[]{:S(2)}) async-start(), calls=%async_computation.2 | async-start | bytes 589824 | tf_op jit(solution)/shard_map/reduce_scatter | solution.py:78
  8.3 26.2 %copy-start.1 = (f32[768,128]{1,0:T(8,128)S(1)}, f32[768,128]{1,0:T(8,128)}, u32[]{:S(2)}) copy-start(f32[768,128]{1,0:T(8,128)} %param.17) | copy-start | bytes 1179652
  83.3 34.2 %copy-start.7 = (s32[128,128]{1,0:T(8,128)S(1)}, s32[128,128]{1,0:T(8,128)}, u32[]{:S(2)}) copy-start(s32[128,128]{1,0:T(8,128)} %param.15) | copy-start | bytes 196612
  87.9 0.8 copy-start.6
  87.9 114.7 %copy-start.9 = (bf16[1024,64]{1,0:T(8,128)(2,1)}, bf16[1024,64]{1,0:T(8,128)(2,1)S(1)}, u32[]{:S(2)}) copy-start(bf16[1024,64]{1,0:T(8,128)(2,1)S(1)} %get-tuple-element.685) | copy-start | bytes 393220
  88.7 113.8 %all-gather.3.cloned.1.call-start = ((), (), s32[]{:S(2)}) async-start(), calls=%async_computation.3 | async-start | bytes 1310720 | tf_op jit(solution)/shard_map/all_gather | solution.py:86
  176.5 119.7 %reduce-scatter.5.cloned.1.call-start = ((), (), s32[]{:S(2)}) async-start(), calls=%async_computation.4 | async-start | bytes 589824 | tf_op jit(solution)/shard_map/reduce_scatter | solution.py:78
  202.6 6.5 %copy-start = (s32[768,128]{1,0:T(8,128)S(1)}, s32[768,128]{1,0:T(8,128)}, u32[]{:S(2)}) copy-start(s32[768,128]{1,0:T(8,128)} %param.16) | copy-start | bytes 1179652
  209.0 38.7 %copy-start.2 = (bf16[768,64]{1,0:T(8,128)(2,1)}, bf16[768,64]{1,0:T(8,128)(2,1)S(1)}, u32[]{:S(2)}) copy-start(bf16[768,64]{1,0:T(8,128)(2,1)S(1)} %get-tuple-element.680) | copy-start | bytes 294916
  209.2 49.3 %copy-start.4 = (f32[1024,128]{1,0:T(8,128)S(1)}, f32[1024,128]{1,0:T(8,128)}, u32[]{:S(2)}) copy-start(f32[1024,128]{1,0:T(8,128)} %custom-call.2) | copy-start | bytes 1572868
  266.0 0.8 copy-start.5
  266.8 114.9 %copy-start.3 = (bf16[768,64]{1,0:T(8,128)(2,1)S(1)}, bf16[768,64]{1,0:T(8,128)(2,1)}, u32[]{:S(2)}) copy-start(bf16[768,64]{1,0:T(8,128)(2,1)} %copy-done.2) | copy-start | bytes 294916
  266.8 114.9 %all-gather.5.cloned.1.call-start = ((), (), s32[]{:S(2)}) async-start(), calls=%async_computation.5 | async-start | bytes 1310720 | tf_op jit(solution)/shard_map/all_gather | solution.py:86
  297.1 84.6 %copy-start.8 = (f32[128,128]{1,0:T(8,128)}, f32[128,128]{1,0:T(8,128)S(1)}, u32[]{:S(2)}) copy-start(f32[128,128]{1,0:T(8,128)S(1)} %get-tuple-element.459) | copy-start | bytes 196612
Sparse Core Ops, SparseCore 0:
  88.8 28.5 reduce-scatter.2
  176.6 25.9 all-gather.2
  266.9 29.2 reduce-scatter.4
  354.4 27.1 all-gather.4
where the time goes:
time: 397 us; the launch traced here: 396 us
  blocking collectives  247 us (62%)
  waiting for transfers between devices  101 us (25%)
  matrix products  24.7 us (6%)
  between operations  14 us (4%)
  other arithmetic  5.16 us (1%)
    pmax x4, blocking collectives, column_peak(): return lax.pmax(jnp.max(values, axis=0), ('blk', 'dom'))  154 us
    reduce_scatter x2, waiting for transfers between devices, body(): lax.psum_scatter(partial_value, 'dom', scatter_dimension=0, tiled=True)  58 us
    all_gather x2, waiting for transfers between devices, body(): lax.all_gather(weights, 'blk', axis=0, tiled=True)  43.1 us
    all_gather x2, blocking collectives, body(): block_logs = lax.all_gather(source_logs, 'dom', axis=0, tiled=True)  36 us
    dot_general x10, matrix products, add_block(): jnp.dot(kernel, weight_piece, preferred_element_type=jnp.float32)  24.7 us
    all_gather x2, blocking collectives, body(): lax.all_gather(scaled, 'blk', axis=0, tiled=True)  21.2 us
    all_gather x1, blocking collectives, body(): lax.all_gather(normalized(source_emb), 'dom', axis=0, tiled=True)  15.4 us
    all_gather x1, blocking collectives, body(): target_group = lax.all_gather(own_targets, 'blk', axis=0, tiled=True)  10.2 us
  transfers between devices with their start and end apart: 4, of which 4 were waited for; matrix products, arithmetic and copies ran while one was open for 0% of the time, Pallas kernels for 0%

commit v1 on v0

v1 whole, which is shorter than its diff:
```python
import functools
import math

import jax
import jax.numpy as jnp
from jax import lax
from jax.experimental import pallas as pl
from jax.experimental.pallas import tpu as pltpu
from jax.sharding import PartitionSpec as P

ITERS = 2
INV_EPS = 20.0
LOG2E = math.log2(math.e)
CHUNK = 128


def normalized(values):
    widened = values.astype(jnp.float32)
    squared = jnp.sum(widened * widened, axis=1, keepdims=True) + 1e-06
    return widened * lax.rsqrt(squared)


def kernel(nb, nz, *refs):
    (semb, temb, scnt, tcnt, warm, sout, tout,
     S, tt, tt2, warm2, peak, K, W, VT, tsT, part_out, part_in, z_out, z_in,
     ts_out, ts_in, ssem, rsem) = refs
    src = semb.shape[0]
    tgt = temb.shape[0]
    cols = warm.shape[1]
    slab = src * nz
    b = lax.axis_index("blk")
    d = lax.axis_index("dom")
    z = d // 2
    c = d % 2
    count = [0]

    core_peer = (b, 2 * z + 1 - c)

    def z_peer(k):
        return (b, 2 * lax.rem(z + k, nz) + c)

    def b_peer(k):
        return (lax.rem(b + k, nb), d)

    started = []

    def send(source, target, device):
        i = count[0]
        count[0] += 1
        copy = pltpu.make_async_remote_copy(
            src_ref=source, dst_ref=target, send_sem=ssem.at[i], recv_sem=rsem.at[i],
            device_id=device, device_id_type=pl.DeviceIdType.MESH)
        copy.start()
        started.append(copy)
        return copy

    barrier = pltpu.get_barrier_semaphore()
    peers = [core_peer] + [z_peer(k) for k in range(1, nz)] + [b_peer(k) for k in range(1, nb)]
    for device in peers:
        pl.semaphore_signal(barrier, inc=1, device_id=device, device_id_type=pl.DeviceIdType.MESH)

    own_block = b * nz + z
    my_rows = pl.ds(pl.multiple_of(own_block * src, src), src)
    S[my_rows, :] = normalized(semb[...]).astype(jnp.bfloat16)
    peak[0] = jnp.broadcast_to(jnp.max(warm[...], axis=0, keepdims=True), (8, cols))
    tt[...] = normalized(temb[...]).T.astype(jnp.bfloat16)
    pl.semaphore_wait(barrier, len(peers))

    emb_z, peak_z = [], []
    for k in range(1, nz):
        emb_z.append(send(S.at[my_rows], S.at[my_rows], z_peer(k)))
        peak_z.append(send(peak.at[0], peak.at[k], z_peer(k)))
    emb_core = send(tt, tt2, core_peer)
    warm_core = send(warm, warm2, core_peer)

    def slab_rows(block):
        return pl.ds(pl.multiple_of(block * slab, slab), slab)

    for copy in peak_z:
        copy.wait_recv()
    top = peak[0]
    for k in range(1, nz):
        top = jnp.maximum(top, peak[k])
    peak[nz] = top
    peak_b = [send(peak.at[nz], peak.at[nz + k], b_peer(k)) for k in range(1, nb)]
    for copy in emb_z:
        copy.wait_recv()
    own_rows = slab_rows(b)
    emb_b = [send(S.at[own_rows], S.at[own_rows], b_peer(k)) for k in range(1, nb)]
    emb_core.wait_recv()

    width = next(w for w in (384, 256, 128) if tgt % w == 0)
    steps = slab // CHUNK
    scale = INV_EPS * LOG2E

    def make_kernel(block, out_slot):
        base = block * slab

        def one(step, carry):
            rows = pl.ds(pl.multiple_of(base + step * CHUNK, CHUNK), CHUNK)
            piece = S[rows, :]
            total = None
            for half, emb in enumerate((tt, tt2)):
                for start in range(0, tgt, width):
                    prod = jnp.dot(piece, emb[:, start:start + width], preferred_element_type=jnp.float32)
                    kern = jnp.exp2((prod - 1.0) * scale).astype(jnp.bfloat16)
                    at = half * tgt + start
                    K[rows, at:at + width] = kern
                    if out_slot is not None:
                        term = jnp.dot(kern, W[at:at + width, :], preferred_element_type=jnp.float32)
                        total = term if total is None else total + term
            if out_slot is not None:
                part_out[out_slot, pl.ds(pl.multiple_of(step * CHUNK, CHUNK), CHUNK), :] = total.astype(jnp.bfloat16)
            return carry

        lax.fori_loop(0, steps, one, 0)

    def source_part(block, out_slot):
        base = block * slab

        def one(step, carry):
            rows = pl.ds(pl.multiple_of(base + step * CHUNK, CHUNK), CHUNK)
            total = jnp.dot(K[rows, :], W[...], preferred_element_type=jnp.float32)
            part_out[out_slot, pl.ds(pl.multiple_of(step * CHUNK, CHUNK), CHUNK), :] = total.astype(jnp.bfloat16)
            return carry

        lax.fori_loop(0, steps, one, 0)

    make_kernel(b, None)

    for copy in peak_b:
        copy.wait_recv()
    top = peak[nz]
    for k in range(1, nb):
        top = jnp.maximum(top, peak[nz + k])
    peak[nz + nb] = top
    peak_core = send(peak.at[nz + nb], peak.at[nz + nb + 1], core_peer)
    warm_core.wait_recv()
    peak_core.wait_recv()
    shift = jnp.maximum(peak[nz + nb], peak[nz + nb + 1])[0:1, :]
    W[0:tgt, :] = jnp.exp(warm[...] - shift).astype(jnp.bfloat16)
    W[tgt:2 * tgt, :] = jnp.exp(warm2[...] - shift).astype(jnp.bfloat16)

    log_ns = math.log(src * nb * nz * 2)
    log_nt = math.log(tgt * nb * nz * 2)
    inv_ns = 1.0 / (src * nb * nz * 2)
    inv_nt = 1.0 / (tgt * nb * nz * 2)

    for it in range(ITERS):
        last = it == ITERS - 1
        slot0 = it * (nb - 1)
        sent = []
        for k in range(1, nb):
            block = lax.rem(b + k, nb)
            slot = slot0 + k - 1
            if it == 0:
                emb_b[nb - k - 1].wait_recv()
                make_kernel(block, it * nb + k)
            else:
                source_part(block, it * nb + k)
            sent.append(send(part_out.at[it * nb + k], part_in.at[slot], b_peer(k)))
        source_part(b, it * nb)
        for copy in sent:
            copy.wait_recv()
        zslot = it * nz

        def summed(block):
            rows = pl.ds(pl.multiple_of(block * src, src), src)
            total = part_out[it * nb, rows, :].astype(jnp.float32)
            for k in range(nb - 1):
                total = total + part_in[slot0 + k, rows, :].astype(jnp.float32)
            return total

        sent = []
        for k in range(1, nz):
            z_out[zslot + k] = summed(lax.rem(z + k, nz)).astype(jnp.bfloat16)
            sent.append(send(z_out.at[zslot + k], z_in.at[zslot + k], z_peer(k)))
        sums = summed(z)
        for copy in sent:
            copy.wait_recv()
        for k in range(1, nz):
            sums = sums + z_in[zslot + k].astype(jnp.float32)
        counts = scnt[...].astype(jnp.float32)
        vt = VT.at[it]
        vt[own_block] = (counts * inv_ns / sums).T.astype(jnp.bfloat16)
        sent = [send(vt.at[own_block], vt.at[own_block], z_peer(k)) for k in range(1, nz)]
        if last:
            sout[...] = jnp.log(counts) - log_ns - shift - jnp.log(sums)
        for copy in sent:
            copy.wait_recv()
        mine = pl.ds(b * nz, nz)
        sent = [send(vt.at[mine], vt.at[mine], b_peer(k)) for k in range(1, nb)]

        def weights(block):
            return jnp.concatenate([vt[block * nz + i] for i in range(nz)], axis=1)

        tsT[...] = jnp.dot(weights(b), K[slab_rows(b), :], preferred_element_type=jnp.float32)
        for k in range(1, nb):
            sent[k - 1].wait_recv()
            block = lax.rem(b - k + nb, nb)
            lhs = weights(block)
            if k < nb - 1:
                tsT[...] += jnp.dot(lhs, K[slab_rows(block), :], preferred_element_type=jnp.float32)
            else:
                ts_out[it] = (tsT[:, tgt:] + jnp.dot(
                    lhs, K[slab_rows(block), tgt:], preferred_element_type=jnp.float32)).astype(jnp.bfloat16)
                across = send(ts_out.at[it], ts_in.at[it], core_peer)
                tsT[:, :tgt] += jnp.dot(lhs, K[slab_rows(block), :tgt], preferred_element_type=jnp.float32)
        across.wait_recv()
        tsums = (tsT[:, :tgt] + ts_in[it].astype(jnp.float32)).T
        tcounts = tcnt[...].astype(jnp.float32)
        if last:
            tout[...] = jnp.log(tcounts) - log_nt + shift - jnp.log(tsums)
        else:
            W2 = W
            W2[0:tgt, :] = (tcounts * inv_nt / tsums).astype(jnp.bfloat16)
            across = send(W2.at[0:tgt], W2.at[tgt:2 * tgt], core_peer)
            across.wait_recv()
    for copy in started:
        copy.wait_send()


def n_copies(nb, nz):
    return 2 * (nz - 1) + 2 + 2 * (nb - 1) + 1 + ITERS * (2 * (nb - 1) + 2 * (nz - 1) + 1) + ITERS - 1


def body(source_emb, target_emb, source_counts, target_counts, warm_start):
    nb = lax.axis_size("blk")
    nz = lax.axis_size("dom") // 2
    src, dim = source_emb.shape
    tgt = target_emb.shape[0]
    cols = warm_start.shape[1]
    slab = src * nz
    copies = n_copies(nb, nz)
    bf = jnp.bfloat16
    f32 = jnp.float32
    vmem = pltpu.VMEM
    pairs = slab * nb * 2 * tgt
    return pl.pallas_call(
        functools.partial(kernel, nb, nz),
        out_shape=(jax.ShapeDtypeStruct((src, cols), f32), jax.ShapeDtypeStruct((tgt, cols), f32)),
        in_specs=[pl.BlockSpec(memory_space=pltpu.VMEM)] * 5,
        out_specs=(pl.BlockSpec(memory_space=pltpu.VMEM),) * 2,
        scratch_shapes=[
            vmem((slab * nb, dim), bf),
            vmem((dim, tgt), bf),
            vmem((dim, tgt), bf),
            vmem((tgt, cols), f32),
            vmem((nz + nb + 2, 8, cols), f32),
            vmem((slab * nb, 2 * tgt), bf),
            vmem((2 * tgt, cols), bf),
            vmem((ITERS, nb * nz, cols, src), bf),
            vmem((cols, 2 * tgt), f32),
            vmem((ITERS * nb, slab, cols), bf),
            vmem((ITERS * (nb - 1), slab, cols), bf),
            vmem((ITERS * nz, src, cols), bf),
            vmem((ITERS * nz, src, cols), bf),
            vmem((ITERS, cols, tgt), bf),
            vmem((ITERS, cols, tgt), bf),
            pltpu.SemaphoreType.DMA((copies,)),
            pltpu.SemaphoreType.DMA((copies,)),
        ],
        cost_estimate=pl.CostEstimate(
            flops=2 * pairs * (dim + 4 * cols), bytes_accessed=2 * 10**6, transcendentals=pairs),
        compiler_params=pltpu.CompilerParams(
            collective_id=0, has_side_effects=True, vmem_limit_bytes=56 * 2**20),
    )(source_emb, target_emb, source_counts, target_counts, warm_start)


def solution(mesh):
    spec = P(("blk", "dom"), None)
    return jax.shard_map(
        body, mesh=mesh, in_specs=(spec,) * 5, out_specs=(spec,) * 2, check_vma=False)
```

time: 397 us -> 80 us (0.20)
  blocking collectives: 247 us -> 0 us
  waiting for transfers between devices: 101 us -> 0 us
  Pallas kernels: 0 us -> 72.7 us
  matrix products: 24.7 us -> 0 us
  between operations: 14 us -> 0.64 us
  other arithmetic: 5.16 us -> 0 us
    pmax x4 -> x0, blocking collectives: 154 us -> none  [column_peak(): return lax.pmax(jnp.max(values, axis=0), ('blk', 'dom'))]
    all_gather x7 -> x0, blocking collectives: 92.5 us -> none  [the longest x2 36 us: body(): block_logs = lax.all_gather(source_logs, 'dom', axis=0, tiled=True)]
    pallas_call x0 -> x1, Pallas kernels: none -> 72.7 us  [body(): pl.pallas_call(functools.partial(kernel, nb, nz), out_shape=(jax.ShapeDty...]
    reduce_scatter x2 -> x0, waiting for transfers between devices: 58 us -> none  [body(): lax.psum_scatter(partial_value, 'dom', scatter_dimension=0, tiled=True)]
    all_gather x2 -> x0, waiting for transfers between devices: 43.1 us -> none  [body(): lax.all_gather(weights, 'blk', axis=0, tiled=True)]
    dot_general x10 -> x0, matrix products: 24.7 us -> none  [add_block(): jnp.dot(kernel, weight_piece, preferred_element_type=jnp.float32)]
  transfers between devices with their start and end apart: 4 -> 0, of which waited for: 4 -> 0; matrix products, arithmetic and copies ran while one was open for 0% -> 0% of each run, Pallas kernels for 0% -> 0%
where the time goes in v1:
time: 80 us; the launch traced here: 79.7 us
  Pallas kernels  72.7 us (91%)
  local copies, waits for them, and re-layouts  6.38 us (8%)
    pallas_call x1, Pallas kernels, body(): pl.pallas_call(functools.partial(kernel, nb, nz), out_shape=(jax.ShapeDty...  72.7 us
    unnamed x4, local copies, waits for them, and re-layouts  6.38 us

profile of v1, /device:TPU:1, one launch (start us, length us, event | category | flops | bytes accessed | tf_op | source)
XLA Modules:
  0.0 79.7 jit_solution(7257611140029666627)
XLA Ops:
  0.6 1.4 %copy.7.refs_0_ = bf16[128,64]{1,0:T(8,128)(2,1)} copy(bf16[128,64]{0,1:T(8,128)(2,1)} %param.5) | data formatting | bytes 32768 | tf_op args[0]
  2.1 1.7 %copy.8.refs_1_ = bf16[768,64]{1,0:T(8,128)(2,1)} copy(bf16[768,64]{0,1:T(8,128)(2,1)} %param.6) | data formatting | bytes 196608 | tf_op args[1]
  3.8 72.7 %shard_map.68 = (f32[128,128]{1,0:T(8,128)}, f32[768,128]{1,0:T(8,128)}) custom-call(bf16[128,64]{1,0:T(8,128)(2,1)} %copy.7.refs_0_, bf16[768,64]{1,0:T(8,128)(2,1)} %copy.8.refs_1_, s32[128,128]{1,0:T(8,128)} %refs_2_.1, s32[768,128]{1,0:T(8,128)} %refs_3_.1, f32[768,128]{1,0:T(8,128)} %refs_4_.1), custom_call_target="tpu_custom_call" | custom-call | flops 3623878656 | bytes 2000000 | tf_op jit(solution)/shard_map/pallas_call | solution.py:239
  76.5 1.5 %copy.11 = f32[128,128]{1,0:T(8,128)} copy(f32[128,128]{1,0:T(8,128)} %get-tuple-element.4) | data formatting | bytes 131072
  78.0 1.8 %copy.12 = f32[768,128]{1,0:T(8,128)} copy(f32[768,128]{1,0:T(8,128)} %get-tuple-element.5) | data formatting | bytes 786432

commit v2 on v1

v2 whole, which is shorter than its diff:
```python
import functools
import math

import jax
import jax.numpy as jnp
from jax import lax
from jax.experimental import pallas as pl
from jax.experimental.pallas import tpu as pltpu
from jax.sharding import PartitionSpec as P

ITERS = 2
INV_EPS = 20.0
LOG2E = math.log2(math.e)


def normalized(values):
    widened = values.astype(jnp.float32)
    squared = jnp.sum(widened * widened, axis=0, keepdims=True) + 1e-06
    return widened * lax.rsqrt(squared)


def kernel(nb, nz, *refs):
    (semb, temb, scnt, tcnt, warm, sout, tout,
     S, tt, tt2, warm2, peak, K, W, VT, tsT, part_out, part_in, z_out, z_in,
     ts_out, ts_in, ssem, rsem) = refs
    src = semb.shape[1]
    tgt = temb.shape[1]
    cols = warm.shape[1]
    group = src * nb
    b = lax.axis_index("blk")
    d = lax.axis_index("dom")
    z = d // 2
    c = d % 2
    count = [0]
    f32, bf = jnp.float32, jnp.bfloat16

    core_peer = (b, 2 * z + 1 - c)

    def z_peer(k):
        return (b, 2 * lax.rem(z + k, nz) + c)

    def b_peer(k):
        return (lax.rem(b + k, nb), d)

    started = []

    def send(source, target, device):
        i = count[0]
        count[0] += 1
        copy = pltpu.make_async_remote_copy(
            src_ref=source, dst_ref=target, send_sem=ssem.at[i], recv_sem=rsem.at[i],
            device_id=device, device_id_type=pl.DeviceIdType.MESH)
        copy.start()
        started.append(copy)
        return copy

    def arrived(copies):
        for copy in copies:
            copy.wait_recv()

    barrier = pltpu.get_barrier_semaphore()
    peers = [core_peer] + [z_peer(k) for k in range(1, nz)] + [b_peer(k) for k in range(1, nb)]
    for device in peers:
        pl.semaphore_signal(barrier, inc=1, device_id=device, device_id_type=pl.DeviceIdType.MESH)

    def group_of(i):
        return lax.rem(z - i + nz, nz)

    def block_rows(i):
        return pl.ds(pl.multiple_of((group_of(i) * nb + b) * src, src), src)

    def group_rows(i):
        return pl.ds(pl.multiple_of(group_of(i) * group, group), group)

    S[block_rows(0), :] = normalized(semb[...]).T.astype(bf)
    peak[0] = jnp.broadcast_to(jnp.max(warm[...], axis=0, keepdims=True), (8, cols))
    tt[...] = normalized(temb[...]).astype(bf)
    pl.semaphore_wait(barrier, len(peers))

    mine = S.at[block_rows(0)]
    emb_z = [send(mine, mine, z_peer(k)) for k in range(1, nz)]
    peak_z = [send(peak.at[0], peak.at[k], z_peer(k)) for k in range(1, nz)]
    emb_core = send(tt, tt2, core_peer)
    emb_b = [[send(mine, mine, b_peer(j)) for j in range(1, nb)]]
    warm_core = send(warm, warm2, core_peer)

    arrived(peak_z)
    top = peak[0]
    for k in range(1, nz):
        top = jnp.maximum(top, peak[k])
    peak[nz] = top
    peak_b = [send(peak.at[nz], peak.at[nz + k], b_peer(k)) for k in range(1, nb)]
    for k in range(1, nz):
        emb_z[k - 1].wait_recv()
        piece = S.at[block_rows(k)]
        emb_b.append([send(piece, piece, b_peer(j)) for j in range(1, nb)])
    emb_core.wait_recv()

    width = 256 if tgt % 256 == 0 else 128
    tall = 256 if group % 256 == 0 else 128
    scale = INV_EPS * LOG2E

    def make_kernel(i):
        base = group_of(i) * group

        def one(step, carry):
            rows = pl.ds(pl.multiple_of(base + step * tall, tall), tall)
            piece = S[rows, :]
            for half, emb in enumerate((tt, tt2)):
                for start in range(0, tgt, width):
                    prod = jnp.dot(piece, emb[:, start:start + width], preferred_element_type=f32)
                    at = half * tgt + start
                    K[rows, at:at + width] = jnp.exp2((prod - 1.0) * scale).astype(bf)
            return carry

        lax.fori_loop(0, group // tall, one, 0)

    arrived(emb_b[0])
    make_kernel(0)
    arrived(peak_b)
    top = peak[nz]
    for k in range(1, nb):
        top = jnp.maximum(top, peak[nz + k])
    peak[nz + nb] = top
    peak_core = send(peak.at[nz + nb], peak.at[nz + nb + 1], core_peer)
    if nz > 1:
        arrived(emb_b[1])
        make_kernel(1)
    warm_core.wait_recv()
    peak_core.wait_recv()
    shift = jnp.maximum(peak[nz + nb], peak[nz + nb + 1])[0:1, :]
    W[0:tgt, :] = jnp.exp(warm[...] - shift).astype(bf)
    W[tgt:2 * tgt, :] = jnp.exp(warm2[...] - shift).astype(bf)

    all_src = src * nb * nz * 2
    all_tgt = tgt * nb * nz * 2

    for it in range(ITERS):
        last = it == ITERS - 1
        to_b = [None] * (nz + 1)

        def scatter(i):
            part = part_out.at[it * nz + i % nz]
            part[...] = jnp.dot(K[group_rows(i), :], W[...], preferred_element_type=f32).astype(bf)
            to_b[i] = []
            for j in range(1, nb):
                rows = pl.ds(pl.multiple_of(lax.rem(b + j, nb) * src, src), src)
                to_b[i].append(send(part.at[rows], part_in.at[(it * nz + i % nz) * (nb - 1) + j - 1], b_peer(j)))

        def summed(i):
            arrived(to_b[i])
            slot = it * nz + i % nz
            total = part_out[slot, pl.ds(pl.multiple_of(b * src, src), src), :].astype(f32)
            for j in range(nb - 1):
                total = total + part_in[slot * (nb - 1) + j].astype(f32)
            return total

        to_z = []

        def pass_on(i):
            slot = it * nz + i
            z_out[slot] = summed(i).astype(bf)
            to_z.append(send(z_out.at[slot], z_in.at[slot], z_peer(nz - i)))

        for i in range(1, nz + 1):
            if it == 0 and 1 < i < nz:
                arrived(emb_b[i])
                make_kernel(i)
            scatter(i)
            if it == 0 and i > 1:
                pass_on(i - 1)
        if it > 0:
            for i in range(1, nz):
                pass_on(i)
        sums = summed(nz)
        arrived(to_z)
        for i in range(1, nz):
            sums = sums + z_in[it * nz + i].astype(f32)
        counts = scnt[...].astype(f32)
        vt = VT.at[it]

        def block(i):
            return vt.at[group_of(i) * nb + b]

        vt[group_of(0) * nb + b] = (counts * (1.0 / all_src) / sums).T.astype(bf)
        from_z = [send(block(0), block(0), z_peer(k)) for k in range(1, nz)]
        from_b = [[send(block(0), block(0), b_peer(j)) for j in range(1, nb)]]
        if last:
            sout[...] = jnp.log(counts) - math.log(all_src) - shift - jnp.log(sums)
        for k in range(1, nz):
            from_z[k - 1].wait_recv()
            from_b.append([send(block(k), block(k), b_peer(j)) for j in range(1, nb)])
        for i in range(nz):
            arrived(from_b[i])
            first = group_of(i) * nb
            lhs = jnp.concatenate([vt[first + j] for j in range(nb)], axis=1)
            for half in (1, 0):
                at = half * tgt
                term = jnp.dot(lhs, K[group_rows(i), at:at + tgt], preferred_element_type=f32)
                if i > 0:
                    term = term + tsT[:, at:at + tgt]
                if i == nz - 1 and half == 1:
                    ts_out[it] = term.astype(bf)
                    across = send(ts_out.at[it], ts_in.at[it], core_peer)
                else:
                    tsT[:, at:at + tgt] = term
        tcounts = tcnt[...].astype(f32)
        across.wait_recv()
        tsums = (tsT[:, :tgt] + ts_in[it].astype(f32)).T
        if last:
            tout[...] = jnp.log(tcounts) - math.log(all_tgt) + shift - jnp.log(tsums)
        else:
            W[0:tgt, :] = (tcounts * (1.0 / all_tgt) / tsums).astype(bf)
            send(W.at[0:tgt], W.at[tgt:2 * tgt], core_peer).wait_recv()
    for copy in started:
        copy.wait_send()


def n_copies(nb, nz):
    gather = (nz - 1) + (nb - 1) * nz
    return gather + (nz - 1) + (nb - 1) + 3 + ITERS * (gather + nz * (nb - 1) + nz - 1 + 1) + ITERS - 1


def place(s_in, t_in, s_out, t_out, sem):
    copies = [pltpu.make_async_copy(s_in, s_out, sem.at[0]), pltpu.make_async_copy(t_in, t_out, sem.at[1])]
    for copy in copies:
        copy.start()
    for copy in copies:
        copy.wait()


def body(source_emb, target_emb, source_counts, target_counts, warm_start):
    nb = lax.axis_size("blk")
    nz = lax.axis_size("dom") // 2
    src, dim = source_emb.shape
    tgt = target_emb.shape[0]
    cols = warm_start.shape[1]
    group = src * nb
    copies = n_copies(nb, nz)
    bf = jnp.bfloat16
    f32 = jnp.float32
    vmem = pltpu.VMEM
    pairs = group * nz * 2 * tgt
    shapes = (jax.ShapeDtypeStruct((src, cols), f32), jax.ShapeDtypeStruct((tgt, cols), f32))
    results = pl.pallas_call(
        functools.partial(kernel, nb, nz),
        out_shape=shapes,
        in_specs=[pl.BlockSpec(memory_space=pltpu.VMEM)] * 5,
        out_specs=(pl.BlockSpec(memory_space=pltpu.VMEM),) * 2,
        scratch_shapes=[
            vmem((group * nz, dim), bf),
            vmem((dim, tgt), bf),
            vmem((dim, tgt), bf),
            vmem((tgt, cols), f32),
            vmem((nz + nb + 2, 8, cols), f32),
            vmem((group * nz, 2 * tgt), bf),
            vmem((2 * tgt, cols), bf),
            vmem((ITERS, nb * nz, cols, src), bf),
            vmem((cols, 2 * tgt), f32),
            vmem((ITERS * nz, group, cols), bf),
            vmem((ITERS * nz * (nb - 1), src, cols), bf),
            vmem((ITERS * nz, src, cols), bf),
            vmem((ITERS * nz, src, cols), bf),
            vmem((ITERS, cols, tgt), bf),
            vmem((ITERS, cols, tgt), bf),
            pltpu.SemaphoreType.DMA((copies,)),
            pltpu.SemaphoreType.DMA((copies,)),
        ],
        cost_estimate=pl.CostEstimate(
            flops=2 * pairs * (dim + 4 * cols), bytes_accessed=2 * 10**6, transcendentals=pairs),
        compiler_params=pltpu.CompilerParams(
            collective_id=0, has_side_effects=True, vmem_limit_bytes=56 * 2**20),
    )(source_emb.T, target_emb.T, source_counts, target_counts, warm_start)
    return pl.pallas_call(
        place,
        out_shape=shapes,
        in_specs=[pl.BlockSpec(memory_space=pltpu.HBM)] * 2,
        out_specs=(pl.BlockSpec(memory_space=pl.ANY),) * 2,
        scratch_shapes=[pltpu.SemaphoreType.DMA((2,))],
    )(*results)


def solution(mesh):
    spec = P(("blk", "dom"), None)
    return jax.shard_map(
        body, mesh=mesh, in_specs=(spec,) * 5, out_specs=(spec,) * 2, check_vma=False)
```

time: 80 us -> 80.8 us (1.010)
  Pallas kernels: 72.7 us -> 80 us
  local copies, waits for them, and re-layouts: 6.38 us -> 0 us
    pallas_call x1 -> x2, Pallas kernels: 72.7 us -> 80 us  [the longest x1 65 us: body(): pl.pallas_call(functools.partial(kernel, nb, nz), out_shape=shapes, in_sp...]
    unnamed x4 -> x0, local copies, waits for them, and re-layouts: 6.38 us -> none
where the time goes in v2:
time: 80.8 us; the launch traced here: 80.7 us
  Pallas kernels  80 us (99%)
    pallas_call x1, Pallas kernels, body(): pl.pallas_call(functools.partial(kernel, nb, nz), out_shape=shapes, in_sp...  65 us
    pallas_call x1, Pallas kernels, body(): pl.pallas_call(place, out_shape=shapes, in_specs=[pl.BlockSpec(memory_spa...  15 us

profile of v2, /device:TPU:1, one launch (start us, length us, event | category | flops | bytes accessed | tf_op | source)
XLA Modules:
  0.0 80.7 jit_solution(10788550856981420004)
XLA Ops:
  0.6 65.0 %shard_map.68 = (f32[128,128]{1,0:T(8,128)}, f32[768,128]{1,0:T(8,128)}) custom-call(bf16[64,128]{1,0:T(8,128)(2,1)} %bitcast.3, bf16[64,768]{1,0:T(8,128)(2,1)} %bitcast.2, s32[128,128]{1,0:T(8,128)} %refs_2_.1, s32[768,128]{1,0:T(8,128)} %refs_3_.1, f32[768,128]{1,0:T(8,128)} %refs_4_.1), custom_call_target="tpu_custom_call" | custom-call | flops 3623878656 | bytes 2000000 | tf_op jit(solution)/shard_map/pallas_call | solution.py:245
  65.6 15.0 %shard_map.69 = (f32[128,128]{1,0:T(8,128)}, f32[768,128]{1,0:T(8,128)}) custom-call(f32[128,128]{1,0:T(8,128)} %get-tuple-element.4.s_in, f32[768,128]{1,0:T(8,128)} %get-tuple-element.5.t_in), custom_call_target="tpu_custom_call" | custom-call | tf_op jit(solution)/shard_map/pallas_call | solution.py:274

commit v3 on v2

--- a/solution.py
+++ b/solution.py
@@ -21,7 +21,7 @@
 
 def kernel(nb, nz, *refs):
     (semb, temb, scnt, tcnt, warm, sout, tout,
-     S, tt, tt2, warm2, peak, K, W, VT, tsT, part_out, part_in, z_out, z_in,
+     S, tt, tt2, warm2, tcnt2, peak, K, W, VT, tsT, part_out, part_in, z_out, z_in,
      ts_out, ts_in, ssem, rsem) = refs
     src = semb.shape[1]
     tgt = temb.shape[1]
@@ -72,9 +72,13 @@
     def group_rows(i):
         return pl.ds(pl.multiple_of(group_of(i) * group, group), group)
 
-    S[block_rows(0), :] = normalized(semb[...]).T.astype(bf)
+    scaled = normalized(semb[...]).astype(bf).astype(f32).T * (INV_EPS * LOG2E)
+    high = scaled.astype(bf)
+    low = (scaled - high.astype(f32)).astype(bf)
+    S[block_rows(0), :] = jnp.concatenate([high, low], axis=1)
     peak[0] = jnp.broadcast_to(jnp.max(warm[...], axis=0, keepdims=True), (8, cols))
-    tt[...] = normalized(temb[...]).astype(bf)
+    unit = normalized(temb[...]).astype(bf)
+    tt[...] = jnp.concatenate([unit, unit], axis=0)
     pl.semaphore_wait(barrier, len(peers))
 
     mine = S.at[block_rows(0)]
@@ -83,6 +87,7 @@
     emb_core = send(tt, tt2, core_peer)
     emb_b = [[send(mine, mine, b_peer(j)) for j in range(1, nb)]]
     warm_core = send(warm, warm2, core_peer)
+    tcnt_core = send(tcnt, tcnt2, core_peer)
 
     arrived(peak_z)
     top = peak[0]
@@ -98,7 +103,6 @@
 
     width = 256 if tgt % 256 == 0 else 128
     tall = 256 if group % 256 == 0 else 128
-    scale = INV_EPS * LOG2E
 
     def make_kernel(i):
         base = group_of(i) * group
@@ -110,7 +114,7 @@
                 for start in range(0, tgt, width):
                     prod = jnp.dot(piece, emb[:, start:start + width], preferred_element_type=f32)
                     at = half * tgt + start
-                    K[rows, at:at + width] = jnp.exp2((prod - 1.0) * scale).astype(bf)
+                    K[rows, at:at + width] = jnp.exp2(prod).astype(bf)
             return carry
 
         lax.fori_loop(0, group // tall, one, 0)
@@ -186,10 +190,11 @@
         from_z = [send(block(0), block(0), z_peer(k)) for k in range(1, nz)]
         from_b = [[send(block(0), block(0), b_peer(j)) for j in range(1, nb)]]
         if last:
-            sout[...] = jnp.log(counts) - math.log(all_src) - shift - jnp.log(sums)
+            sout[...] = jnp.log(counts) - math.log(all_src) - shift - (jnp.log(sums) - INV_EPS)
         for k in range(1, nz):
             from_z[k - 1].wait_recv()
             from_b.append([send(block(k), block(k), b_peer(j)) for j in range(1, nb)])
+        across = []
         for i in range(nz):
             arrived(from_b[i])
             first = group_of(i) * nb
@@ -199,34 +204,36 @@
                 term = jnp.dot(lhs, K[group_rows(i), at:at + tgt], preferred_element_type=f32)
                 if i > 0:
                     term = term + tsT[:, at:at + tgt]
-                if i == nz - 1 and half == 1:
-                    ts_out[it] = term.astype(bf)
-                    across = send(ts_out.at[it], ts_in.at[it], core_peer)
-                else:
+                if i == nz - 1 and (half == 1 or not last):
+                    ts_out[it, half] = term.astype(bf)
+                    across.append(send(ts_out.at[it, half], ts_in.at[it, 1 - half], core_peer))
+                if half == 0 or i < nz - 1 or not last:
                     tsT[:, at:at + tgt] = term
-        tcounts = tcnt[...].astype(f32)
-        across.wait_recv()
-        tsums = (tsT[:, :tgt] + ts_in[it].astype(f32)).T
         if last:
-            tout[...] = jnp.log(tcounts) - math.log(all_tgt) + shift - jnp.log(tsums)
+            log_counts = jnp.log(tcnt[...].astype(f32))
+            arrived(across)
+            tsums = (tsT[:, :tgt] + ts_in[it, 0].astype(f32)).T
+            tout[...] = log_counts - math.log(all_tgt) + shift - jnp.log(tsums)
         else:
-            W[0:tgt, :] = (tcounts * (1.0 / all_tgt) / tsums).astype(bf)
-            send(W.at[0:tgt], W.at[tgt:2 * tgt], core_peer).wait_recv()
+            if it == 0:
+                tcnt_core.wait_recv()
+            arrived(across)
+            for half, held in enumerate((tcnt, tcnt2)):
+                at = half * tgt
+                tsums = (tsT[:, at:at + tgt] + ts_in[it, half].astype(f32)).T
+                W[at:at + tgt, :] = (held[...].astype(f32) * (1.0 / all_tgt) / tsums).astype(bf)
     for copy in started:
         copy.wait_send()
 
 
 def n_copies(nb, nz):
     gather = (nz - 1) + (nb - 1) * nz
-    return gather + (nz - 1) + (nb - 1) + 3 + ITERS * (gather + nz * (nb - 1) + nz - 1 + 1) + ITERS - 1
-
-
-def place(s_in, t_in, s_out, t_out, sem):
-    copies = [pltpu.make_async_copy(s_in, s_out, sem.at[0]), pltpu.make_async_copy(t_in, t_out, sem.at[1])]
-    for copy in copies:
-        copy.start()
-    for copy in copies:
-        copy.wait()
+    return gather + (nz - 1) + (nb - 1) + 4 + ITERS * (gather + nz * (nb - 1) + nz - 1 + 1) + ITERS - 1
+
+
+def place(s_in, t_in, s_out, t_out):
+    s_out[...] = s_in[...]
+    t_out[...] = t_in[...]
 
 
 def body(source_emb, target_emb, source_counts, target_counts, warm_start):
@@ -248,10 +255,11 @@
         in_specs=[pl.BlockSpec(memory_space=pltpu.VMEM)] * 5,
         out_specs=(pl.BlockSpec(memory_space=pltpu.VMEM),) * 2,
         scratch_shapes=[
-            vmem((group * nz, dim), bf),
-            vmem((dim, tgt), bf),
-            vmem((dim, tgt), bf),
+            vmem((group * nz, 2 * dim), bf),
+            vmem((2 * dim, tgt), bf),
+            vmem((2 * dim, tgt), bf),
             vmem((tgt, cols), f32),
+            vmem((tgt, cols), target_counts.dtype),
             vmem((nz + nb + 2, 8, cols), f32),
             vmem((group * nz, 2 * tgt), bf),
             vmem((2 * tgt, cols), bf),
@@ -261,8 +269,8 @@
             vmem((ITERS * nz * (nb - 1), src, cols), bf),
             vmem((ITERS * nz, src, cols), bf),
             vmem((ITERS * nz, src, cols), bf),
-            vmem((ITERS, cols, tgt), bf),
-            vmem((ITERS, cols, tgt), bf),
+            vmem((ITERS, 2, cols, tgt), bf),
+            vmem((ITERS, 2, cols, tgt), bf),
             pltpu.SemaphoreType.DMA((copies,)),
             pltpu.SemaphoreType.DMA((copies,)),
         ],
@@ -274,9 +282,8 @@
     return pl.pallas_call(
         place,
         out_shape=shapes,
-        in_specs=[pl.BlockSpec(memory_space=pltpu.HBM)] * 2,
-        out_specs=(pl.BlockSpec(memory_space=pl.ANY),) * 2,
-        scratch_shapes=[pltpu.SemaphoreType.DMA((2,))],
+        in_specs=[pl.BlockSpec(memory_space=pltpu.VMEM)] * 2,
+        out_specs=(pl.BlockSpec(memory_space=pltpu.VMEM),) * 2,
     )(*results)
 
 

time: 80.8 us -> 66.2 us (0.82)
  Pallas kernels: 80 us -> 65.4 us
    pallas_call x1, Pallas kernels: 15 us -> 1.81 us  [body(): pl.pallas_call(place, out_shape=shapes, in_specs=[pl.BlockSpec(memory_spa...]
    pallas_call x1, Pallas kernels: 65 us -> 63.6 us  [body(): pl.pallas_call(functools.partial(kernel, nb, nz), out_shape=shapes, in_sp...]
where the time goes in v3:
time: 66.2 us; the launch traced here: 66.1 us
  Pallas kernels  65.4 us (99%)
    pallas_call x1, Pallas kernels, body(): pl.pallas_call(functools.partial(kernel, nb, nz), out_shape=shapes, in_sp...  63.6 us
    pallas_call x1, Pallas kernels, body(): pl.pallas_call(place, out_shape=shapes, in_specs=[pl.BlockSpec(memory_spa...  1.81 us

profile of v3, /device:TPU:1, one launch (start us, length us, event | category | flops | bytes accessed | tf_op | source)
XLA Modules:
  0.0 66.1 jit_solution(16746821723675680816)
XLA Ops:
  0.6 63.6 %shard_map.68 = (f32[128,128]{1,0:T(8,128)}, f32[768,128]{1,0:T(8,128)}) custom-call(bf16[64,128]{1,0:T(8,128)(2,1)} %bitcast.3, bf16[64,768]{1,0:T(8,128)(2,1)} %bitcast.2, s32[128,128]{1,0:T(8,128)} %refs_2_.1, s32[768,128]{1,0:T(8,128)} %refs_3_.1, f32[768,128]{1,0:T(8,128)} %refs_4_.1), custom_call_target="tpu_custom_call" | custom-call | flops 3623878656 | bytes 2000000 | tf_op jit(solution)/shard_map/pallas_call | solution.py:252
  64.2 1.8 %shard_map.69 = (f32[128,128]{1,0:T(8,128)}, f32[768,128]{1,0:T(8,128)}) custom-call(f32[128,128]{1,0:T(8,128)} %get-tuple-element.4.s_in, f32[768,128]{1,0:T(8,128)} %get-tuple-element.5.t_in), custom_call_target="tpu_custom_call" | custom-call | tf_op jit(solution)/shard_map/pallas_call | solution.py:282

commit v4 on v3

--- a/solution.py
+++ b/solution.py
@@ -69,6 +69,42 @@
     def block_rows(i):
         return pl.ds(pl.multiple_of((group_of(i) * nb + b) * src, src), src)
 
+    square = nb == 4
+    if square:
+        y, x = b // 2, b % 2
+        first_b = 2 * (y + c * (1 - 2 * y)) + x + (1 - c) * (1 - 2 * x)
+        second_b = 2 * (y + (1 - c) * (1 - 2 * y)) + x + c * (1 - 2 * x)
+        corner_b = 3 - b
+
+    def gather(from_z, block):
+        pending = []
+        relays = []
+
+        def spread(i):
+            piece = block(i, b)
+            if not square:
+                pending.append([send(piece, piece, b_peer(j)) for j in range(1, nb)])
+                return
+            relays.append(send(piece, piece, (first_b, d)))
+            pending.append([send(piece, piece, (second_b, d))])
+
+        def relay(i):
+            if square:
+                relays[i].wait_recv()
+                piece = block(i, first_b)
+                pending[i].append(send(piece, piece, (second_b, d)))
+
+        spread(0)
+        for k in range(1, nz):
+            from_z[k - 1].wait_recv()
+            spread(k)
+            relay(k - 1)
+        relay(nz - 1)
+        return pending
+
+    def source_block(i, bb):
+        return S.at[pl.ds(pl.multiple_of((group_of(i) * nb + bb) * src, src), src)]
+
     def group_rows(i):
         return pl.ds(pl.multiple_of(group_of(i) * group, group), group)
 
@@ -85,7 +121,6 @@
     emb_z = [send(mine, mine, z_peer(k)) for k in range(1, nz)]
     peak_z = [send(peak.at[0], peak.at[k], z_peer(k)) for k in range(1, nz)]
     emb_core = send(tt, tt2, core_peer)
-    emb_b = [[send(mine, mine, b_peer(j)) for j in range(1, nb)]]
     warm_core = send(warm, warm2, core_peer)
     tcnt_core = send(tcnt, tcnt2, core_peer)
 
@@ -95,10 +130,7 @@
         top = jnp.maximum(top, peak[k])
     peak[nz] = top
     peak_b = [send(peak.at[nz], peak.at[nz + k], b_peer(k)) for k in range(1, nb)]
-    for k in range(1, nz):
-        emb_z[k - 1].wait_recv()
-        piece = S.at[block_rows(k)]
-        emb_b.append([send(piece, piece, b_peer(j)) for j in range(1, nb)])
+    emb_b = gather(emb_z, source_block)
     emb_core.wait_recv()
 
     width = 256 if tgt % 256 == 0 else 128
@@ -143,19 +175,36 @@
         last = it == ITERS - 1
         to_b = [None] * (nz + 1)
 
+        def rows_of(bb):
+            return pl.ds(pl.multiple_of(bb * src, src), src)
+
         def scatter(i):
             part = part_out.at[it * nz + i % nz]
             part[...] = jnp.dot(K[group_rows(i), :], W[...], preferred_element_type=f32).astype(bf)
+            base = (it * nz + i % nz) * (nb - 1)
+            if square:
+                to_b[i] = [send(part.at[rows_of(corner_b)], part_in.at[base], (second_b, d)),
+                           send(part.at[rows_of(second_b)], part_in.at[base + 1], (second_b, d))]
+                return
             to_b[i] = []
             for j in range(1, nb):
-                rows = pl.ds(pl.multiple_of(lax.rem(b + j, nb) * src, src), src)
-                to_b[i].append(send(part.at[rows], part_in.at[(it * nz + i % nz) * (nb - 1) + j - 1], b_peer(j)))
+                to_b[i].append(send(part.at[rows_of(lax.rem(b + j, nb))], part_in.at[base + j - 1], b_peer(j)))
+
+        def combine(i):
+            if not square:
+                return
+            slot = it * nz + i % nz
+            to_b[i].pop(0).wait_recv()
+            rows = rows_of(first_b)
+            both = part_out[slot, rows, :].astype(f32) + part_in[slot * (nb - 1)].astype(f32)
+            part_out[slot, rows, :] = both.astype(bf)
+            to_b[i].append(send(part_out.at[slot, rows], part_in.at[slot * (nb - 1) + 2], (first_b, d)))
 
         def summed(i):
             arrived(to_b[i])
             slot = it * nz + i % nz
-            total = part_out[slot, pl.ds(pl.multiple_of(b * src, src), src), :].astype(f32)
-            for j in range(nb - 1):
+            total = part_out[slot, rows_of(b), :].astype(f32)
+            for j in range(1 if square else 0, nb - 1):
                 total = total + part_in[slot * (nb - 1) + j].astype(f32)
             return total
 
@@ -171,11 +220,16 @@
                 arrived(emb_b[i])
                 make_kernel(i)
             scatter(i)
-            if it == 0 and i > 1:
-                pass_on(i - 1)
+            if i > 1:
+                combine(i - 1)
+            if it == 0 and i > 2:
+                pass_on(i - 2)
         if it > 0:
-            for i in range(1, nz):
+            for i in range(1, nz - 1):
                 pass_on(i)
+        combine(nz)
+        if nz > 1:
+            pass_on(nz - 1)
         sums = summed(nz)
         arrived(to_z)
         for i in range(1, nz):
@@ -183,17 +237,14 @@
         counts = scnt[...].astype(f32)
         vt = VT.at[it]
 
-        def block(i):
-            return vt.at[group_of(i) * nb + b]
+        def weight_block(i, bb):
+            return vt.at[group_of(i) * nb + bb]
 
         vt[group_of(0) * nb + b] = (counts * (1.0 / all_src) / sums).T.astype(bf)
-        from_z = [send(block(0), block(0), z_peer(k)) for k in range(1, nz)]
-        from_b = [[send(block(0), block(0), b_peer(j)) for j in range(1, nb)]]
+        from_z = [send(weight_block(0, b), weight_block(0, b), z_peer(k)) for k in range(1, nz)]
+        from_b = gather(from_z, weight_block)
         if last:
             sout[...] = jnp.log(counts) - math.log(all_src) - shift - (jnp.log(sums) - INV_EPS)
-        for k in range(1, nz):
-            from_z[k - 1].wait_recv()
-            from_b.append([send(block(k), block(k), b_peer(j)) for j in range(1, nb)])
         across = []
         for i in range(nz):
             arrived(from_b[i])

time: 66.2 us -> 80 us (1.21)
  Pallas kernels: 65.4 us -> 79.2 us
    pallas_call x1, Pallas kernels: 63.6 us -> 77.4 us  [body(): pl.pallas_call(functools.partial(kernel, nb, nz), out_shape=shapes, in_sp...]
where the time goes in v4:
time: 80 us; the launch traced here: 79.9 us
  Pallas kernels  79.2 us (99%)
    pallas_call x1, Pallas kernels, body(): pl.pallas_call(functools.partial(kernel, nb, nz), out_shape=shapes, in_sp...  77.4 us
    pallas_call x1, Pallas kernels, body(): pl.pallas_call(place, out_shape=shapes, in_specs=[pl.BlockSpec(memory_spa...  1.81 us

profile of v4, /device:TPU:1, one launch (start us, length us, event | category | flops | bytes accessed | tf_op | source)
XLA Modules:
  0.0 79.9 jit_solution(4007599672356461165)
XLA Ops:
  0.6 77.4 %shard_map.68 = (f32[128,128]{1,0:T(8,128)}, f32[768,128]{1,0:T(8,128)}) custom-call(bf16[64,128]{1,0:T(8,128)(2,1)} %bitcast.3, bf16[64,768]{1,0:T(8,128)(2,1)} %bitcast.2, s32[128,128]{1,0:T(8,128)} %refs_2_.1, s32[768,128]{1,0:T(8,128)} %refs_3_.1, f32[768,128]{1,0:T(8,128)} %refs_4_.1), custom_call_target="tpu_custom_call" | custom-call | flops 3623878656 | bytes 2000000 | tf_op jit(solution)/shard_map/pallas_call | solution.py:303
  78.1 1.8 %shard_map.69 = (f32[128,128]{1,0:T(8,128)}, f32[768,128]{1,0:T(8,128)}) custom-call(f32[128,128]{1,0:T(8,128)} %get-tuple-element.4.s_in, f32[768,128]{1,0:T(8,128)} %get-tuple-element.5.t_in), custom_call_target="tpu_custom_call" | custom-call | tf_op jit(solution)/shard_map/pallas_call | solution.py:333

commit v5 on v3

--- a/solution.py
+++ b/solution.py
@@ -171,11 +171,10 @@
                 arrived(emb_b[i])
                 make_kernel(i)
             scatter(i)
-            if it == 0 and i > 1:
-                pass_on(i - 1)
-        if it > 0:
-            for i in range(1, nz):
-                pass_on(i)
+            if it == 0 and i > 2:
+                pass_on(i - 2)
+        for i in range(max(1, nz - 1) if it == 0 else 1, nz):
+            pass_on(i)
         sums = summed(nz)
         arrived(to_z)
         for i in range(1, nz):

time: 66.2 us -> 64 us (0.967)
  Pallas kernels: 65.4 us -> 63.2 us
    pallas_call x1, Pallas kernels: 63.6 us -> 61.4 us  [body(): pl.pallas_call(functools.partial(kernel, nb, nz), out_shape=shapes, in_sp...]
where the time goes in v5:
time: 64 us; the launch traced here: 63.8 us
  Pallas kernels  63.2 us (99%)
  between operations  0.64 us (1%)
    pallas_call x1, Pallas kernels, body(): pl.pallas_call(functools.partial(kernel, nb, nz), out_shape=shapes, in_sp...  61.4 us
    pallas_call x1, Pallas kernels, body(): pl.pallas_call(place, out_shape=shapes, in_specs=[pl.BlockSpec(memory_spa...  1.81 us

profile of v5, /device:TPU:1, one launch (start us, length us, event | category | flops | bytes accessed | tf_op | source)
XLA Modules:
  0.0 63.8 jit_solution(17954442537806474500)
XLA Ops:
  0.6 61.4 %shard_map.68 = (f32[128,128]{1,0:T(8,128)}, f32[768,128]{1,0:T(8,128)}) custom-call(bf16[64,128]{1,0:T(8,128)(2,1)} %bitcast.3, bf16[64,768]{1,0:T(8,128)(2,1)} %bitcast.2, s32[128,128]{1,0:T(8,128)} %refs_2_.1, s32[768,128]{1,0:T(8,128)} %refs_3_.1, f32[768,128]{1,0:T(8,128)} %refs_4_.1), custom_call_target="tpu_custom_call" | custom-call | flops 3623878656 | bytes 2000000 | tf_op jit(solution)/shard_map/pallas_call | solution.py:251
  62.0 1.8 %shard_map.69 = (f32[128,128]{1,0:T(8,128)}, f32[768,128]{1,0:T(8,128)}) custom-call(f32[128,128]{1,0:T(8,128)} %get-tuple-element.4.s_in, f32[768,128]{1,0:T(8,128)} %get-tuple-element.5.t_in), custom_call_target="tpu_custom_call" | custom-call | tf_op jit(solution)/shard_map/pallas_call | solution.py:281
